TPU v7x, 32 devices: a whole 2x2x4 slice. The times are simulated.
32 devices in a mesh: tile: 8 (over y, x, core), agent: 4 (over z).
Axes of the slice: x: 2, y: 2, z: 4, core: 2. Of those that a mesh axis runs over, the one named last changes fastest.
Arguments:
- agent_state: float32 [4, 1, 16, 128, 256], P(None, None, None, 'tile', 'agent'), may hold values from 0 to 2
- measured: float32 [1, 16, 8192], P(None, None, ('tile', 'agent')), may hold values from 0 to 12
- bin_index: int32 [16, 128, 256], P(None, 'tile', 'agent'), may hold values from 64 to 446, as said below
- bin_frac: int32 [16, 128, 256], P(None, 'tile', 'agent'), may hold values from 0 to 723, as said below
- patch_offsets: int32 [3], replicated, may hold values from 1 to 15
- agent_weights: float32 [4], replicated, may hold values from 0.5 to 2
- up_weight: bfloat16 [3, 256, 4096], P(None, None, 'agent'), may hold values from -0.375 to 0.375
- down_weight: bfloat16 [3, 4096, 256], P(None, 'agent'), may hold values from -0.09375 to 0.09375
Outputs:
- state_next: float32 [4, 1, 16, 128, 256], P(None, None, None, 'tile', 'agent')
- data_fit: float32 [1, 16, 128, 256], P(None, None, 'tile', 'agent')
Inputs may be any that keep to these rules, and one draw needn't show every extreme that they name: bin_index[a, x, y] = floor(((x - 64) c_a + (y - 128) s_a) / 724) + 256 and bin_frac[a, x, y] is the remainder of that division, for whole numbers c_a, s_a of size at most 724 with c_a * c_a + s_a * s_a close to 524176, one pair an angle. bin_frac is the remainder that belongs to bin_index.
All inputs are finite; a program needn't handle non-finite values.
Results may differ from a plain program's by a relative error of at most 0.0003.
The roundings to bfloat16 on the way count: a program that leaves them out, or rounds other values in their place, can miss the bound.
Values may be sent and summed in bfloat16 or wider, within the bound.
A program may use at most 64 MiB of HBM per device.

v0:
```python
import functools
import math

import jax
import jax.numpy as jnp
from jax import lax
from jax.experimental import pallas as pl
from jax.experimental.pallas import tpu as pltpu
from jax.sharding import PartitionSpec as P

PATCH = 16
LANES = 128
DENOM = 724.0


def split_pair(values):
    high = values.astype(jnp.bfloat16)
    low = (values - high.astype(jnp.float32)).astype(jnp.bfloat16)
    return high, low


def interpolation_rows(low_ref, frac_ref, angle, start, window):
    lows = low_ref[pl.ds(angle, 1), :] - start
    near = frac_ref[pl.ds(angle, 1), :].astype(jnp.float32) / DENOM
    far = 1.0 - near
    near_high = near.astype(jnp.bfloat16).astype(jnp.float32)
    far_high = far.astype(jnp.bfloat16).astype(jnp.float32)
    near_low, far_low = near - near_high, far - far_high
    apart = lax.broadcasted_iota(jnp.int32, (window, lows.shape[1]), 0) - lows
    at_near, at_far = apart == 0, apart == 1
    high = jnp.where(at_near, near_high, jnp.where(at_far, far_high, 0.0))
    low = jnp.where(at_near, near_low, jnp.where(at_far, far_low, 0.0))
    return jnp.concatenate([high.astype(jnp.bfloat16), low.astype(jnp.bfloat16)], axis=0)


def project_kernel(factor, window, starts_ref, volume_ref, low_ref, frac_ref, sino_ref):
    angles, planes, bins = sino_ref.shape
    high, low = split_pair(volume_ref[...])
    stacked = jnp.concatenate([high, low], axis=0)

    def step(angle, carry):
        start = starts_ref[angle]
        rows = interpolation_rows(low_ref, frac_ref, angle, start, window)
        out = lax.dot_general(
            stacked, rows, (((1,), (1,)), ((), ())), preferred_element_type=jnp.float32
        )
        out = out[:planes] + out[planes:]
        out = factor * (out[:, :window] + out[:, window:])
        if bins > window:
            out = jnp.concatenate([out, jnp.zeros((planes, bins - window), jnp.float32)], axis=1)
            out = pltpu.roll(out, start, 1)
        sino_ref[angle] = out
        return carry

    lax.fori_loop(0, angles, step, 0, unroll=4)


def spread_kernel(factor, window, starts_ref, misfit_ref, low_ref, frac_ref, volume_ref, out_ref):
    angles, planes, bins = misfit_ref.shape
    out_ref[...] = volume_ref[...]

    def step(angle, carry):
        start = starts_ref[angle]
        rows = interpolation_rows(low_ref, frac_ref, angle, start, window)
        resid = misfit_ref[angle]
        if bins > window:
            resid = pltpu.roll(resid, bins - start, 1)[:, :window]
        high, low = split_pair(resid)
        left = jnp.concatenate([high, low], axis=0)
        left = jnp.concatenate([left, left], axis=1)
        out = jnp.dot(left, rows, preferred_element_type=jnp.float32)
        out_ref[...] -= factor * (out[:planes] + out[planes:])
        return carry

    lax.fori_loop(0, angles, step, 0, unroll=4)


def exchange_kernel(
    chunks_ref, target_ref, patches_ref, up_ref, down_ref, misfit_ref, nets_ref,
    tile_parts, band, agent_parts, every, wide, terms, term_parts,
    tile_send, tile_recv, sum_send, sum_recv, own_send, own_recv,
    every_send, every_recv, patch_send, patch_recv, term_send, term_recv,
):
    tiles, agents = chunks_ref.shape[0], chunks_ref.shape[1]
    tile, agent = lax.axis_index("tile"), lax.axis_index("agent")

    def tile_at(step):
        return lax.rem(tile + step, tiles)

    def agent_at(step):
        return lax.rem(agent + step, agents)

    def copy(source, target, send, recv, step, to):
        return pltpu.make_async_remote_copy(
            src_ref=source,
            dst_ref=target,
            send_sem=send.at[step],
            recv_sem=recv.at[step],
            device_id=to,
            device_id_type=pl.DeviceIdType.MESH,
        )

    def to_tile(step):
        return (tile_at(step), agent)

    def to_agent(step):
        return (tile, agent_at(step))

    def over(count, body):
        def step_body(step, carry):
            body(step)
            return carry

        lax.fori_loop(1, count, step_body, 0)

    barrier = pltpu.get_barrier_semaphore()
    over(agents, lambda step: pl.semaphore_signal(
        barrier, inc=1, device_id=to_agent(step), device_id_type=pl.DeviceIdType.MESH))
    over(tiles, lambda step: pl.semaphore_signal(
        barrier, inc=1, device_id=to_tile(step), device_id_type=pl.DeviceIdType.MESH))
    pl.semaphore_wait(barrier, tiles + agents - 2)

    def tile_copy(step):
        return copy(
            chunks_ref.at[tile_at(step)], tile_parts.at[step], tile_send, tile_recv, step,
            to_tile(step))

    def patch_copy(which):
        return lambda step: copy(
            patches_ref.at[which], wide.at[which, step], patch_send.at[which],
            patch_recv.at[which], step, to_agent(step))

    def sum_copy(step):
        return copy(
            band.at[agent_at(step)], agent_parts.at[step], sum_send, sum_recv, step,
            to_agent(step))

    def own_copy(step):
        return copy(
            every.at[tile, agent], every.at[tile, agent], own_send, own_recv, step,
            to_agent(step))

    def own_arrival(step):
        where = every.at[tile, agent_at(agents - step)]
        return copy(where, where, own_send, own_recv, step, to_agent(step))

    def every_copy(step):
        return copy(
            every.at[tile], every.at[tile], every_send, every_recv, step, to_tile(step))

    def every_arrival(step):
        where = every.at[tile_at(tiles - step)]
        return copy(where, where, every_send, every_recv, step, to_tile(step))

    def term_copy(which):
        return lambda step: copy(
            terms.at[which, agents - step], term_parts.at[which, step], term_send.at[which],
            term_recv.at[which], step, to_agent(step))

    nets = range(patches_ref.shape[0])
    over(tiles, lambda step: tile_copy(step).start())
    for which in nets:
        over(agents, lambda step: patch_copy(which)(step).start())
        wide[which, 0] = patches_ref[which]
    band[...] = chunks_ref[tile]

    def add_tile(step):
        tile_copy(step).wait_recv()
        band[...] += tile_parts[step]

    over(tiles, add_tile)
    over(agents, lambda step: sum_copy(step).start())
    every[tile, agent] = band[agent] - target_ref[...]

    def add_agent(step):
        sum_copy(step).wait_recv()
        every[tile, agent] += agent_parts[step]

    over(agents, add_agent)
    over(agents, lambda step: own_copy(step).start())

    count = patches_ref.shape[1]
    for which in nets:
        over(agents, lambda step: patch_copy(which)(step).wait_recv())
        rows = wide[which].reshape(agents * count, patches_ref.shape[2])
        hidden = jnp.dot(rows, up_ref[which], preferred_element_type=jnp.float32)
        hidden = jnp.maximum(hidden, 0.0).astype(jnp.bfloat16)
        out = jnp.dot(hidden, down_ref[which], preferred_element_type=jnp.float32)
        terms[which] = out.reshape(agents, count, out.shape[1])
        over(agents, lambda step: term_copy(which)(step).start())

    over(agents, lambda step: own_arrival(step).wait_recv())
    over(tiles, lambda step: every_copy(step).start())
    over(tiles, lambda step: every_arrival(step).wait_recv())
    misfit_ref[...] = every[...]
    for which in nets:
        nets_ref[which] = terms[which, 0]

        def add_terms(step):
            term_copy(which)(step).wait_recv()
            nets_ref[which] += term_parts[which, step]

        over(agents, add_terms)
    over(tiles, lambda step: tile_copy(step).wait_send())
    for which in nets:
        over(agents, lambda step: patch_copy(which)(step).wait_send())
        over(agents, lambda step: term_copy(which)(step).wait_send())
    over(agents, lambda step: sum_copy(step).wait_send())
    over(agents, lambda step: own_copy(step).wait_send())
    over(tiles, lambda step: every_copy(step).wait_send())


def exchange(chunks, target, patches, up_weight, down_weight):
    tiles, agents, planes, own = chunks.shape
    whole = pl.BlockSpec(memory_space=pltpu.VMEM)
    nets = jax.ShapeDtypeStruct(patches.shape, jnp.float32)
    sems = [pltpu.SemaphoreType.DMA((n,)) for n in (
        tiles, tiles, agents, agents, agents, agents, tiles, tiles)]
    sems += [pltpu.SemaphoreType.DMA((patches.shape[0], agents))] * 4
    by_net = (patches.shape[0], agents) + patches.shape[1:]
    return pl.pallas_call(
        exchange_kernel,
        out_shape=(jax.ShapeDtypeStruct(chunks.shape, jnp.float32), nets),
        in_specs=[whole] * 5,
        out_specs=(whole, whole),
        scratch_shapes=[
            pltpu.VMEM(chunks.shape, jnp.float32),
            pltpu.VMEM((agents, planes, own), jnp.float32),
            pltpu.VMEM((agents, planes, own), jnp.float32),
            pltpu.VMEM(chunks.shape, jnp.float32),
            pltpu.VMEM(by_net, jnp.bfloat16),
            pltpu.VMEM(by_net, jnp.float32),
            pltpu.VMEM(by_net, jnp.float32),
            *sems,
        ],
        compiler_params=pltpu.CompilerParams(
            collective_id=0, has_side_effects=True, vmem_limit_bytes=48 * 2**20
        ),
        name="exchange",
    )(chunks, target, patches, up_weight, down_weight)


def permute(block, step_tile, step_agent):
    tiles, agents = lax.axis_size("tile"), lax.axis_size("agent")
    pairs = []
    for tile in range(tiles):
        for agent in range(agents):
            source = (tile + step_tile) % tiles * agents + (agent + step_agent) % agents
            pairs.append((source, tile * agents + agent))
    return lax.ppermute(block, ("tile", "agent"), pairs)


def pad_lanes(block):
    short = -block.shape[-1] % LANES
    return jnp.pad(block, ((0, 0),) * (block.ndim - 1) + ((0, short),))


def ahead_kernel(offsets_ref, both_ref, rows_ref, cols_ref, out_ref):
    planes, rows, cols = out_ref.shape[1:]

    def ahead(block, shift, axis):
        return pltpu.roll(block, block.shape[axis] - shift, axis)

    first = ahead(both_ref[...], offsets_ref[0], 1)[:, :rows]
    first = ahead(first, offsets_ref[0], 2)
    second = ahead(rows_ref[...], offsets_ref[1], 1)
    third = ahead(cols_ref[...], offsets_ref[2], 2)
    out_ref[0] = first[:, :, :cols].astype(out_ref.dtype)
    out_ref[1] = second[:, :rows, :cols].astype(out_ref.dtype)
    out_ref[2] = third[:, :, :cols].astype(out_ref.dtype)


def make_patches(noisy, offsets):
    times, slices, rows, cols = noisy.shape[1:]
    row_blocks, col_blocks = rows // PATCH, cols // PATCH
    flat = noisy.reshape(3, times * slices, rows, cols)
    below = permute(flat[:2, :, :PATCH], 1, 0)
    sides = jnp.stack([flat[0, :, :, :PATCH], flat[2, :, :, :PATCH]])
    beyond = permute(sides, 0, 1)
    corner = permute(flat[0, :, :PATCH, :PATCH], 1, 1)
    top = jnp.concatenate([flat[0], beyond[0]], axis=2)
    bottom = jnp.concatenate([below[0], corner], axis=2)
    both = pad_lanes(jnp.concatenate([top, bottom], axis=1).astype(jnp.float32))
    tall = pad_lanes(jnp.concatenate([flat[1], below[1]], axis=1).astype(jnp.float32))
    broad = pad_lanes(jnp.concatenate([flat[2], beyond[1]], axis=2).astype(jnp.float32))
    vmem = pl.BlockSpec(memory_space=pltpu.VMEM)
    moved = pl.pallas_call(
        ahead_kernel,
        out_shape=jax.ShapeDtypeStruct(flat.shape, jnp.bfloat16),
        in_specs=[pl.BlockSpec(memory_space=pltpu.SMEM), vmem, vmem, vmem],
        out_specs=vmem,
        compiler_params=pltpu.CompilerParams(vmem_limit_bytes=32 * 2**20),
        name="ahead",
    )(offsets, both, tall, broad)
    first = moved[0].reshape(times, slices, row_blocks, PATCH, col_blocks, PATCH)
    first = first.transpose(0, 1, 2, 4, 3, 5).reshape(-1, PATCH * PATCH)
    second = moved[1].reshape(times, slices, row_blocks, PATCH, cols)
    second = second.transpose(0, 2, 4, 1, 3).reshape(-1, slices * PATCH)
    third = moved[2].reshape(times, slices, rows, col_blocks, PATCH)
    third = third.transpose(0, 2, 3, 1, 4).reshape(-1, slices * PATCH)
    return jnp.stack([first, second, third])


def join_kernel(offsets_ref, weights_ref, state_ref, fit_ref, both_ref, rows_ref, cols_ref, out_ref):
    planes, rows, cols = fit_ref.shape

    def back(block, shift, axis):
        return pltpu.roll(block, block.shape[axis] - (PATCH - shift), axis)

    first = back(both_ref[...], offsets_ref[0], 1)[:, :rows]
    first = back(first, offsets_ref[0], 2)[:, :, :cols]
    second = back(rows_ref[...], offsets_ref[1], 1)[:, :rows, :cols]
    third = back(cols_ref[...], offsets_ref[2], 2)[:, :, :cols]
    answers = [fit_ref[...]]
    for which, removed in enumerate((first, second, third)):
        answers.append(state_ref[which + 1] - removed)
    total = weights_ref[0]
    for which in range(1, len(answers)):
        total = total + weights_ref[which]
    joined = jnp.zeros_like(answers[0])
    for which, answer in enumerate(answers):
        share = jnp.full(joined.shape, weights_ref[which]) / jnp.full(joined.shape, total)
        joined = joined + share * (2.0 * answer - state_ref[which])
    for which, answer in enumerate(answers):
        out_ref[which] = state_ref[which] + joined - answer


def spread_nets(nets, shape):
    times, slices, rows, cols = shape
    row_blocks, col_blocks = rows // PATCH, cols // PATCH
    flat = (times * slices, rows, cols)
    first = nets[0].reshape(times, slices, row_blocks, col_blocks, PATCH, PATCH)
    first = first.transpose(0, 1, 2, 4, 3, 5).reshape(flat)
    second = nets[1].reshape(times, row_blocks, cols, slices, PATCH)
    second = second.transpose(0, 3, 1, 4, 2).reshape(flat)
    third = nets[2].reshape(times, rows, col_blocks, slices, PATCH)
    third = third.transpose(0, 3, 1, 2, 4).reshape(flat)
    low_row, low_col = rows - PATCH, cols - PATCH
    above = permute(jnp.stack([first[:, low_row:], second[:, low_row:]]), -1, 0)
    before = permute(jnp.stack([first[:, :, low_col:], third[:, :, low_col:]]), 0, -1)
    corner = permute(first[:, low_row:, low_col:], -1, -1)
    top = jnp.concatenate([corner, above[0]], axis=2)
    bottom = jnp.concatenate([before[0], first], axis=2)
    both = pad_lanes(jnp.concatenate([top, bottom], axis=1))
    tall = pad_lanes(jnp.concatenate([above[1], second], axis=1))
    broad = pad_lanes(jnp.concatenate([before[1], third], axis=2))
    return both, tall, broad


def join(offsets, weights, state, data_fit, both, tall, broad):
    agents, times, slices, rows, cols = state.shape
    vmem = pl.BlockSpec(memory_space=pltpu.VMEM)
    smem = pl.BlockSpec(memory_space=pltpu.SMEM)
    flat = state.reshape(agents, times * slices, rows, cols)
    out = pl.pallas_call(
        join_kernel,
        out_shape=jax.ShapeDtypeStruct(flat.shape, jnp.float32),
        in_specs=[smem, smem, vmem, vmem, vmem, vmem, vmem],
        out_specs=vmem,
        compiler_params=pltpu.CompilerParams(vmem_limit_bytes=32 * 2**20),
        name="join",
    )(offsets, weights, flat, data_fit.reshape(flat.shape[1:]), both, tall, broad)
    return out.reshape(state.shape)


def data_and_nets(
    volume, bin_index, bin_frac, measured, factor, patches, up_weight, down_weight
):
    angles = bin_index.shape[0]
    planes = volume.shape[0] * volume.shape[1]
    current = volume.reshape(planes, -1)
    tiles, agents, own = lax.axis_size("tile"), lax.axis_size("agent"), measured.shape[2]
    bins = tiles * agents * own // angles
    window = -(-(bin_index.shape[1] + bin_index.shape[2] + 2) // LANES) * LANES
    window = min(window, bins)
    lows = bin_index.reshape(angles, -1)
    fracs = bin_frac.reshape(angles, -1)
    corners = bin_index[:, :: bin_index.shape[1] - 1, :: bin_index.shape[2] - 1]
    starts = jnp.minimum(jnp.min(corners, axis=(1, 2)), bins - window)
    whole = pl.BlockSpec(memory_space=pltpu.VMEM)
    scalars = pl.BlockSpec(memory_space=pltpu.SMEM)
    cost = pl.CostEstimate(
        flops=4 * angles * window * current.shape[1] * planes * 2,
        bytes_accessed=3 * current.size * 4,
        transcendentals=0,
    )
    grant = pltpu.CompilerParams(vmem_limit_bytes=48 * 2**20)
    sino = pl.pallas_call(
        functools.partial(project_kernel, factor, window),
        out_shape=jax.ShapeDtypeStruct((angles, planes, bins), jnp.float32),
        in_specs=[scalars, whole, whole, whole],
        out_specs=whole,
        cost_estimate=cost,
        compiler_params=grant,
        name="project",
    )(starts, current, lows, fracs)
    chunks = jnp.transpose(sino, (1, 0, 2)).reshape(planes, tiles, agents, own)
    chunks = jnp.transpose(chunks, (1, 2, 0, 3))
    misfit, nets = exchange(
        chunks, measured.reshape(planes, own), patches, up_weight, down_weight
    )
    by_angle = jnp.transpose(misfit, (2, 0, 1, 3)).reshape(planes, angles, bins)
    by_angle = jnp.transpose(by_angle, (1, 0, 2))
    result = pl.pallas_call(
        functools.partial(spread_kernel, factor, window),
        out_shape=jax.ShapeDtypeStruct(current.shape, jnp.float32),
        in_specs=[scalars, whole, whole, whole, whole],
        out_specs=whole,
        cost_estimate=cost,
        compiler_params=grant,
        name="spread",
    )(starts, by_angle, lows, fracs, current)
    return result.reshape(volume.shape), nets


def shards(
    agent_state, measured, bin_index, bin_frac, patch_offsets, agent_weights, up_weight, down_weight
):
    row_count = agent_state.shape[3]
    col_count = agent_state.shape[4]
    tile_count = lax.axis_size("tile")
    agent_count = lax.axis_size("agent")
    full_rows = row_count * tile_count
    full_cols = col_count * agent_count
    angles = bin_index.shape[0]
    factor = 1.0 / math.sqrt(angles * (full_rows + full_cols))
    patches = make_patches(agent_state[1:].astype(jnp.bfloat16), patch_offsets)
    data_fit, nets = data_and_nets(
        agent_state[0], bin_index, bin_frac, measured, factor, patches, up_weight, down_weight
    )
    parts = spread_nets(nets, agent_state.shape[1:])
    state_next = join(patch_offsets, agent_weights, agent_state, data_fit, *parts)
    return (state_next, data_fit)


def solution(mesh):
    placed = (
        P(None, None, None, "tile", "agent"),
        P(None, None, ("tile", "agent")),
        P(None, "tile", "agent"),
        P(None, "tile", "agent"),
        P(),
        P(),
        P(None, None, "agent"),
        P(None, "agent", None),
    )
    return jax.shard_map(
        shards,
        mesh=mesh,
        in_specs=placed,
        out_specs=(P(None, None, None, "tile", "agent"), P(None, None, "tile", "agent")),
        check_vma=False,
    )
```

profile of v0, /device:TPU:0, one launch (start us, length us, event | category | flops | bytes accessed | tf_op | source)
XLA Modules:
  0.0 77.6 jit_solution(3302188202743380761)
XLA Ops:
  0.6 0.0 copy-start
  0.6 0.0 copy-start.6
  0.7 1.2 %bitcast_convert_fusion = bf16[4,1,16,16,64]{4,3,2,0,1:T(8,128)(2,1)S(1)} fusion(f32[4,1,16,16,64]{4,3,2,1,0:T(8,128)} %param.8), kind=kLoop, calls=%fused_computation | loop fusion | flops 65536 | bytes 393216 | tf_op jit(solution)/shard_map/convert.6
  1.8 0.0 copy-start.7
  1.8 0.0 slice-start
  1.9 6.4 %collective-permute-start.2 = (bf16[16,16,16]{2,1,0:T(8,128)(2,1)S(1)}, bf16[16,16,16]{2,1,0:T(8,128)(2,1)S(1)}, u32[]{:S(2)}, u32[]{:S(2)}) collective-permute-start(bf16[16,16,16]{2,1,0:T(8,128)(2,1)S(1)} %get-tuple-element.23), channel_id=1, source_target_pairs={{5,0},{6,1},{7,2},{4,3},{9,4},{10,5},{11,6},{8,7},{13,8},{14,9},{1... | collective-permute-start | bytes 24584 | tf_op jit(solution)/shard_map/ppermute | solution.py:250
  8.3 0.5 collective-permute-start
  8.9 0.6 collective-permute-start.1
  9.5 0.0 copy-done.6
  9.5 0.1 slice.88
  9.6 0.1 reshape.48.low_ref
  9.7 0.0 copy-done
  9.7 0.4 reduce_min.9
  10.1 0.0 copy-done.7
  10.1 0.1 reshape.49.frac_ref
  10.3 0.1 reshape_squeeze.21.volume_ref
  10.4 4.8 %project.1 = f32[16,16,512]{2,1,0:T(8,128)S(1)} custom-call(s32[16]{0:T(128)S(1)} %broadcast_minimum_fusion.starts_ref, f32[16,1024]{1,0:T(8,128)S(1)} %reshape_squeeze.21.volume_ref, s32[16,1024]{1,0:T(8,128)S(1)} %reshape.48.low_ref, s32[16,1024]{1,0:T(8,128)S(1)} %reshape.49.frac_ref), custom_call_target="tpu_custom_call" | custom-call | flops 268435456 | bytes 196608 | tf_op jit(solution)/shard_map/project/pallas_call | solution.py:388
  15.2 0.3 copy.19
  15.5 0.2 reshape.50
  15.7 0.0 copy-start.4
  15.8 0.3 copy.41
  16.1 0.0 collective-permute-done
  16.1 0.1 fusion.16.cols_ref
  16.2 0.0 collective-permute-done.1
  16.3 0.0 collective-permute-done.2
  16.3 0.1 fusion.9.both_ref
  16.4 0.7 ahead.1
  17.1 0.0 copy-start.1
  17.1 0.0 copy-start.3
  17.2 0.1 copy.25
  17.3 0.2 reshape_squeeze.22
  17.4 0.8 copy.43
  18.2 1.2 %stack_reshape.15 = bf16[1,64,256]{2,1,0:T(8,128)(2,1)S(1)} reshape(bf16[1,16,1,4,16,16]{5,4,3,1,2,0:T(8,128)(2,1)} %bitcast.102) | data formatting | bytes 65536 | tf_op jit(solution)/shard_map/stack;reshape | solution.py:301
  19.4 0.2 reshape_squeeze.24
  19.6 0.9 %copy.42 = bf16[1,16,16,4,16]{4,1,3,2,0:T(8,128)(2,1)} copy(bf16[1,16,16,4,16]{4,3,2,1,0:T(4,128)(2,1)S(1)} %reshape_squeeze.24) | data formatting | bytes 65536 | tf_op jit(solution)/shard_map/reshape;squeeze | solution.py:299
  20.4 1.2 %stack_reshape.17 = bf16[1,64,256]{2,1,0:T(8,128)(2,1)S(1)} reshape(bf16[1,16,4,16,16]{4,3,2,1,0:T(8,128)(2,1)} %bitcast.103) | data formatting | bytes 65536 | tf_op jit(solution)/shard_map/stack;reshape | solution.py:301
  21.7 0.0 copy-start.2
  21.7 1.4 %copy-done.2 = bf16[3,1024,256]{2,1,0:T(8,128)(2,1)S(1)} copy-done((bf16[3,1024,256]{2,1,0:T(8,128)(2,1)S(1)}, bf16[3,1024,256]{2,1,0:T(8,128)(2,1)}, u32[]{:S(2)}) %copy-start.2) | copy-done | bytes 1572888
  23.1 33.4 %exchange.1 = (f32[8,4,16,256]{3,2,1,0:T(8,128)S(1)}, f32[3,64,256]{2,1,0:T(8,128)S(1)}) custom-call(f32[8,4,16,256]{3,2,1,0:T(8,128)S(1)} %bitcast.92, f32[16,256]{1,0:T(8,128)S(1)} %bitcast.96, bf16[3,64,256]{2,1,0:T(8,128)(2,1)S(1)} %pad_maximum_fusion.3.patches_ref, bf16[3,256,1024]{2,1,0:T(8,128)(2,1)S(1)} %copy-done.1, bf16[3,1024,256]{2,1,0:T(8,128)(2,1)S(1)} %copy-done.2), custom_call_target="tpu_custom_call" | custom-call | tf_op jit(solution)/shard_map/exchange/pallas_call | solution.py:221
  56.5 0.3 copy.26
  56.8 0.3 reshape.53
  57.1 0.3 copy.40
  57.4 4.6 %spread.1 = f32[16,1024]{1,0:T(8,128)S(1)} custom-call(s32[16]{0:T(128)S(1)} %broadcast_minimum_fusion.starts_ref, f32[16,16,512]{2,1,0:T(8,128)S(1)} %bitcast.93, s32[16,1024]{1,0:T(8,128)S(1)} %reshape.48.low_ref, s32[16,1024]{1,0:T(8,128)S(1)} %reshape.49.frac_ref, f32[16,1024]{1,0:T(8,128)S(1)} %reshape_squeeze.21.volume_ref), custom_call_target="tpu_custom_call" | custom-call | flops 268435456 | bytes 196608 | tf_op jit(solution)/shard_map/spread/pallas_call | solution.py:404
  62.0 0.7 reshape.58
  62.8 0.1 reshape_reshape.3.fit_ref
  62.9 0.2 reshape_squeeze.25
  63.1 0.2 copy.39
  63.3 0.3 reshape.54
  63.5 0.3 stack_reshape.18
  63.8 0.1 copy.29
  63.9 0.2 reshape_squeeze.27
  64.1 0.2 copy.38
  64.3 0.3 reshape.55
  64.6 0.1 slice_bitcast_fusion.4
  64.7 0.1 fusion.20
  64.8 0.1 collective-permute-start.3
  64.9 1.3 %collective-permute-start.5 = (f32[2,16,16,16]{3,2,1,0:T(8,128)S(1)}, f32[2,16,16,16]{3,2,1,0:T(8,128)S(1)}, u32[]{:S(2)}, u32[]{:S(2)}) collective-permute-start(f32[2,16,16,16]{3,2,1,0:T(8,128)S(1)} %pad_maximum_fusion.1), channel_id=1, source_target_pairs={{3,0},{0,1},{1,2},{2,3},{7,4},{4,5},{5,6},{6,7},{11,8},{8,9},{9,10... | collective-permute-start | bytes 98312 | tf_op jit(solution)/shard_map/ppermute | solution.py:250
  66.2 1.0 %collective-permute-start.4 = (f32[2,16,16,64]{3,2,1,0:T(8,128)S(1)}, f32[2,16,16,64]{3,2,1,0:T(8,128)S(1)}, u32[]{:S(2)}, u32[]{:S(2)}) collective-permute-start(f32[2,16,16,64]{3,2,1,0:T(8,128)S(1)} %pad_maximum_fusion), channel_id=1, source_target_pairs={{28,0},{29,1},{30,2},{31,3},{0,4},{1,5},{2,6},{3,7},{4,8},{5,9},{6... | collective-permute-start | bytes 393224 | tf_op jit(solution)/shard_map/ppermute | solution.py:250
  67.2 8.4 %collective-permute-done.5 = f32[2,16,16,16]{3,2,1,0:T(8,128)S(1)} collective-permute-done((f32[2,16,16,16]{3,2,1,0:T(8,128)S(1)}, f32[2,16,16,16]{3,2,1,0:T(8,128)S(1)}, u32[]{:S(2)}, u32[]{:S(2)}) %collective-permute-start.5) | collective-permute-done | bytes 32800 | tf_op jit(solution)/shard_map/ppermute | solution.py:250
  75.7 0.1 select_maximum_fusion.3.cols_ref
  75.8 0.0 collective-permute-done.4
  75.9 0.0 collective-permute-done.3
  75.9 0.1 fusion.both_ref
  76.1 1.5 %join.1 = f32[4,16,16,64]{3,2,1,0:T(8,128)} custom-call(s32[3]{0:T(128)S(1)} %copy-done.4, f32[4]{0:T(128)S(1)} %copy-done.5, f32[4,16,16,64]{3,2,1,0:T(8,128)S(1)} %bitcast.91, f32[16,16,64]{2,1,0:T(8,128)S(1)} %reshape_reshape.3.fit_ref, f32[16,32,128]{2,1,0:T(8,128)S(1)} %fusion.both_ref, f32[16,32,128]{2,1,0:T(8,128)S(1)} %select_maximum_fusion.rows_ref, ...), custom_call_target="tpu_custom_call" | custom-call | tf_op jit(solution)/shard_map/join/pallas_call | solution.py:355
  (25 shorter events, 0.4 us)
Async XLA Ops:
  0.6 9.1 %copy-start = (f32[4,1,16,16,64]{4,3,2,1,0:T(8,128)S(1)}, f32[4,1,16,16,64]{4,3,2,1,0:T(8,128)}, u32[]{:S(2)}) copy-start(f32[4,1,16,16,64]{4,3,2,1,0:T(8,128)} %param.8) | copy-start | bytes 786436
  0.6 8.8 %copy-start.6 = (s32[16,16,64]{2,1,0:T(8,128)S(1)}, s32[16,16,64]{2,1,0:T(8,128)}, u32[]{:S(2)}) copy-start(s32[16,16,64]{2,1,0:T(8,128)} %param.10) | copy-start | bytes 196612
  1.8 8.3 %copy-start.7 = (s32[16,16,64]{2,1,0:T(8,128)S(1)}, s32[16,16,64]{2,1,0:T(8,128)}, u32[]{:S(2)}) copy-start(s32[16,16,64]{2,1,0:T(8,128)} %param.11) | copy-start | bytes 196612
  1.8 8.4 %slice-start = ((f32[4,1,16,16,64]{4,3,2,1,0:T(8,128)}), f32[1,1,16,16,64]{4,3,2,1,0:T(8,128)S(1)}, s32[]{:S(2)}) async-start(f32[4,1,16,16,64]{4,3,2,1,0:T(8,128)} %param.8), calls=%async_computation | async-start | bytes 262144 | tf_op jit(solution)/shard_map/slice | solution.py:429
  1.9 14.4 %collective-permute-start.2 = (bf16[16,16,16]{2,1,0:T(8,128)(2,1)S(1)}, bf16[16,16,16]{2,1,0:T(8,128)(2,1)S(1)}, u32[]{:S(2)}, u32[]{:S(2)}) collective-permute-start(bf16[16,16,16]{2,1,0:T(8,128)(2,1)S(1)} %get-tuple-element.23), channel_id=1, source_target_pairs={{5,0},{6,1},{7,2},{4,3},{9,4},{10,5},{11,6},{8,7},{13,8},{14,9},{1... | collective-permute-start | bytes 24584 | tf_op jit(solution)/shard_map/ppermute | solution.py:250
  8.3 7.7 %collective-permute-start = (bf16[2,16,16,16]{3,2,1,0:T(8,128)(2,1)S(1)}, bf16[2,16,16,16]{3,2,1,0:T(8,128)(2,1)S(1)}, u32[]{:S(2)}, u32[]{:S(2)}) collective-permute-start(bf16[2,16,16,16]{3,2,1,0:T(8,128)(2,1)S(1)} %pad_maximum_fusion.2), channel_id=1, source_target_pairs={{1,0},{2,1},{3,2},{0,3},{5,4},{6,5},{7,6},{4,7},{9,8},{10,9},{11,1... | collective-permute-start | bytes 49160 | tf_op jit(solution)/shard_map/ppermute | solution.py:250
  8.9 7.3 %collective-permute-start.1 = (bf16[2,16,16,64]{3,2,1,0:T(8,128)(2,1)S(1)}, bf16[2,16,16,64]{3,2,1,0:T(8,128)(2,1)S(1)}, u32[]{:S(2)}, u32[]{:S(2)}) collective-permute-start(bf16[2,16,16,64]{3,2,1,0:T(8,128)(2,1)S(1)} %slice_bitcast_fusion.6), channel_id=1, source_target_pairs={{4,0},{5,1},{6,2},{7,3},{8,4},{9,5},{10,6},{11,7},{12,8},{13,9},{1... | collective-permute-start | bytes 196616 | tf_op jit(solution)/shard_map/ppermute | solution.py:250
  15.7 0.7 copy-start.4
  17.1 4.5 %copy-start.1 = (bf16[3,256,1024]{2,1,0:T(8,128)(2,1)S(1)}, bf16[3,256,1024]{2,1,0:T(8,128)(2,1)}, u32[]{:S(2)}) copy-start(bf16[3,256,1024]{2,1,0:T(8,128)(2,1)} %up_ref.1) | copy-start | bytes 4718596
  17.1 4.5 %copy-start.3 = (f32[1,16,256]{2,1,0:T(8,128)S(1)}, f32[1,16,256]{2,1,0:T(8,128)}, u32[]{:S(2)}) copy-start(f32[1,16,256]{2,1,0:T(8,128)} %param.9) | copy-start | bytes 49156
  21.7 1.4 %copy-start.2 = (bf16[3,1024,256]{2,1,0:T(8,128)(2,1)S(1)}, bf16[3,1024,256]{2,1,0:T(8,128)(2,1)}, u32[]{:S(2)}) copy-start(bf16[3,1024,256]{2,1,0:T(8,128)(2,1)} %down_ref.1) | copy-start | bytes 4718596
  64.8 11.1 %collective-permute-start.3 = (f32[16,16,16]{2,1,0:T(8,128)S(1)}, f32[16,16,16]{2,1,0:T(8,128)S(1)}, u32[]{:S(2)}, u32[]{:S(2)}) collective-permute-start(f32[16,16,16]{2,1,0:T(8,128)S(1)} %get-tuple-element.25), channel_id=1, source_target_pairs={{31,0},{28,1},{29,2},{30,3},{3,4},{0,5},{1,6},{2,7},{7,8},{4,9},{5... | collective-permute-start | bytes 49160 | tf_op jit(solution)/shard_map/ppermute | solution.py:250
  64.9 10.8 %collective-permute-start.5 = (f32[2,16,16,16]{3,2,1,0:T(8,128)S(1)}, f32[2,16,16,16]{3,2,1,0:T(8,128)S(1)}, u32[]{:S(2)}, u32[]{:S(2)}) collective-permute-start(f32[2,16,16,16]{3,2,1,0:T(8,128)S(1)} %pad_maximum_fusion.1), channel_id=1, source_target_pairs={{3,0},{0,1},{1,2},{2,3},{7,4},{4,5},{5,6},{6,7},{11,8},{8,9},{9,10... | collective-permute-start | bytes 98312 | tf_op jit(solution)/shard_map/ppermute | solution.py:250
  66.2 9.9 %copy-start.5 = (f32[4]{0:T(128)S(1)}, f32[4]{0:T(128)}, u32[]{:S(2)}) copy-start(f32[4]{0:T(128)} %weights_ref.1) | copy-start | bytes 52
  66.2 9.6 %collective-permute-start.4 = (f32[2,16,16,64]{3,2,1,0:T(8,128)S(1)}, f32[2,16,16,64]{3,2,1,0:T(8,128)S(1)}, u32[]{:S(2)}, u32[]{:S(2)}) collective-permute-start(f32[2,16,16,64]{3,2,1,0:T(8,128)S(1)} %pad_maximum_fusion), channel_id=1, source_target_pairs={{28,0},{29,1},{30,2},{31,3},{0,4},{1,5},{2,6},{3,7},{4,8},{5,9},{6... | collective-permute-start | bytes 393224 | tf_op jit(solution)/shard_map/ppermute | solution.py:250
where the time goes:
time: 78.8 us; the launch traced here: 77.6 us
  Pallas kernels  45 us (57%)
  local copies, waits for them, and re-layouts  10.9 us (14%)
  starting transfers between devices  9.96 us (13%)
  waiting for transfers between devices  8.46 us (11%)
  other arithmetic  2.18 us (3%)
  between operations  1.09 us (1%)
    pallas_call x1, Pallas kernels, exchange(): pl.pallas_call(exchange_kernel, out_shape=(jax.ShapeDtypeStruct(chunks.sh...  33.4 us
    ppermute x6, starting transfers between devices, permute(): return lax.ppermute(block, ('tile', 'agent'), pairs)  9.96 us
    ppermute x6, waiting for transfers between devices, permute(): return lax.ppermute(block, ('tile', 'agent'), pairs)  8.46 us
    pallas_call x1, Pallas kernels, data_and_nets(): pl.pallas_call(functools.partial(project_kernel, factor, window), out_sha...  4.8 us
    pallas_call x1, Pallas kernels, data_and_nets(): pl.pallas_call(functools.partial(spread_kernel, factor, window), out_shap...  4.59 us
    another operation x3, local copies, waits for them, and re-layouts, make_patches(): return jnp.stack([first, second, third])  2.52 us
  transfers between devices with their start and end apart: 6, of which 1 were waited for; matrix products, arithmetic and copies ran while one was open for 3% of the time, Pallas kernels for 6%

commit v1 on v0

--- a/solution.py
+++ b/solution.py
@@ -76,10 +76,12 @@
 
 
 def exchange_kernel(
-    chunks_ref, target_ref, patches_ref, up_ref, down_ref, misfit_ref, nets_ref,
+    chunks_ref, target_ref, patches_ref, up_ref, down_ref,
+    misfit_ref, both_ref, rows_ref, cols_ref,
     tile_parts, band, agent_parts, every, wide, terms, term_parts,
     tile_send, tile_recv, sum_send, sum_recv, own_send, own_recv,
     every_send, every_recv, patch_send, patch_recv, term_send, term_recv,
+    edge_send, edge_recv,
 ):
     tiles, agents = chunks_ref.shape[0], chunks_ref.shape[1]
     tile, agent = lax.axis_index("tile"), lax.axis_index("agent")
@@ -118,7 +120,10 @@
         barrier, inc=1, device_id=to_agent(step), device_id_type=pl.DeviceIdType.MESH))
     over(tiles, lambda step: pl.semaphore_signal(
         barrier, inc=1, device_id=to_tile(step), device_id_type=pl.DeviceIdType.MESH))
-    pl.semaphore_wait(barrier, tiles + agents - 2)
+    pl.semaphore_signal(
+        barrier, inc=1, device_id=(tile_at(tiles - 1), agent_at(agents - 1)),
+        device_id_type=pl.DeviceIdType.MESH)
+    pl.semaphore_wait(barrier, tiles + agents - 1)
 
     def tile_copy(step):
         return copy(
@@ -193,14 +198,43 @@
     over(tiles, lambda step: every_copy(step).start())
     over(tiles, lambda step: every_arrival(step).wait_recv())
     misfit_ref[...] = every[...]
+    row_blocks, col_blocks = both_ref.shape[0] - 1, both_ref.shape[1] - 1
+    next_tile, next_agent = to_tile(1), to_agent(1)
+    across = (next_tile[0], next_agent[1])
+    inner_rows, inner_cols = pl.ds(1, row_blocks), pl.ds(1, col_blocks)
+    edges = (
+        (
+            (both_ref.at[row_blocks, inner_cols], both_ref.at[0, inner_cols], 0, next_tile),
+            (both_ref.at[inner_rows, col_blocks], both_ref.at[inner_rows, 0], 1, next_agent),
+            (both_ref.at[row_blocks, col_blocks], both_ref.at[0, 0], 2, across),
+        ),
+        ((rows_ref.at[row_blocks], rows_ref.at[0], 3, next_tile),),
+        ((cols_ref.at[col_blocks], cols_ref.at[0], 4, next_agent),),
+    )
+
+    def edge_copies(which):
+        return [copy(source, target, edge_send, edge_recv, step, to)
+                for source, target, step, to in edges[which]]
+
     for which in nets:
-        nets_ref[which] = terms[which, 0]
 
         def add_terms(step):
             term_copy(which)(step).wait_recv()
-            nets_ref[which] += term_parts[which, step]
+            terms[which, 0] += term_parts[which, step]
 
         over(agents, add_terms)
+        total = terms[which, 0]
+        if which == 0:
+            both_ref[1:, 1:] = total.reshape((row_blocks, col_blocks) + both_ref.shape[2:])
+        elif which == 1:
+            rows_ref[1:] = total.reshape((row_blocks,) + rows_ref.shape[1:])
+        else:
+            cols_ref[1:] = total.reshape((col_blocks,) + cols_ref.shape[1:])
+        for edge in edge_copies(which):
+            edge.start()
+    for which in nets:
+        for edge in edge_copies(which):
+            edge.wait()
     over(tiles, lambda step: tile_copy(step).wait_send())
     for which in nets:
         over(agents, lambda step: patch_copy(which)(step).wait_send())
@@ -210,19 +244,26 @@
     over(tiles, lambda step: every_copy(step).wait_send())
 
 
-def exchange(chunks, target, patches, up_weight, down_weight):
+def exchange(chunks, target, patches, up_weight, down_weight, row_blocks, col_blocks):
     tiles, agents, planes, own = chunks.shape
     whole = pl.BlockSpec(memory_space=pltpu.VMEM)
-    nets = jax.ShapeDtypeStruct(patches.shape, jnp.float32)
+    count, pixels = patches.shape[1:]
+    shapes = (
+        (row_blocks + 1, col_blocks + 1, count // (row_blocks * col_blocks), pixels),
+        (row_blocks + 1, count // row_blocks, pixels),
+        (col_blocks + 1, count // col_blocks, pixels),
+    )
+    parts = tuple(jax.ShapeDtypeStruct(shape, jnp.float32) for shape in shapes)
     sems = [pltpu.SemaphoreType.DMA((n,)) for n in (
         tiles, tiles, agents, agents, agents, agents, tiles, tiles)]
     sems += [pltpu.SemaphoreType.DMA((patches.shape[0], agents))] * 4
+    sems += [pltpu.SemaphoreType.DMA((5,))] * 2
     by_net = (patches.shape[0], agents) + patches.shape[1:]
     return pl.pallas_call(
         exchange_kernel,
-        out_shape=(jax.ShapeDtypeStruct(chunks.shape, jnp.float32), nets),
+        out_shape=(jax.ShapeDtypeStruct(chunks.shape, jnp.float32),) + parts,
         in_specs=[whole] * 5,
-        out_specs=(whole, whole),
+        out_specs=(whole,) * 4,
         scratch_shapes=[
             pltpu.VMEM(chunks.shape, jnp.float32),
             pltpu.VMEM((agents, planes, own), jnp.float32),
@@ -286,19 +327,19 @@
     vmem = pl.BlockSpec(memory_space=pltpu.VMEM)
     moved = pl.pallas_call(
         ahead_kernel,
-        out_shape=jax.ShapeDtypeStruct(flat.shape, jnp.bfloat16),
+        out_shape=jax.ShapeDtypeStruct(flat.shape, jnp.float32),
         in_specs=[pl.BlockSpec(memory_space=pltpu.SMEM), vmem, vmem, vmem],
         out_specs=vmem,
         compiler_params=pltpu.CompilerParams(vmem_limit_bytes=32 * 2**20),
         name="ahead",
     )(offsets, both, tall, broad)
-    first = moved[0].reshape(times, slices, row_blocks, PATCH, col_blocks, PATCH)
-    first = first.transpose(0, 1, 2, 4, 3, 5).reshape(-1, PATCH * PATCH)
+    first = moved[0].reshape(times * slices, row_blocks, PATCH, col_blocks, PATCH)
+    first = first.transpose(1, 3, 0, 2, 4).reshape(-1, PATCH * PATCH)
     second = moved[1].reshape(times, slices, row_blocks, PATCH, cols)
-    second = second.transpose(0, 2, 4, 1, 3).reshape(-1, slices * PATCH)
+    second = second.transpose(2, 0, 4, 1, 3).reshape(-1, slices * PATCH)
     third = moved[2].reshape(times, slices, rows, col_blocks, PATCH)
-    third = third.transpose(0, 2, 3, 1, 4).reshape(-1, slices * PATCH)
-    return jnp.stack([first, second, third])
+    third = third.transpose(3, 0, 2, 1, 4).reshape(-1, slices * PATCH)
+    return jnp.stack([first, second, third]).astype(jnp.bfloat16)
 
 
 def join_kernel(offsets_ref, weights_ref, state_ref, fit_ref, both_ref, rows_ref, cols_ref, out_ref):
@@ -327,24 +368,15 @@
 
 def spread_nets(nets, shape):
     times, slices, rows, cols = shape
-    row_blocks, col_blocks = rows // PATCH, cols // PATCH
-    flat = (times * slices, rows, cols)
-    first = nets[0].reshape(times, slices, row_blocks, col_blocks, PATCH, PATCH)
-    first = first.transpose(0, 1, 2, 4, 3, 5).reshape(flat)
-    second = nets[1].reshape(times, row_blocks, cols, slices, PATCH)
-    second = second.transpose(0, 3, 1, 4, 2).reshape(flat)
-    third = nets[2].reshape(times, rows, col_blocks, slices, PATCH)
-    third = third.transpose(0, 3, 1, 2, 4).reshape(flat)
-    low_row, low_col = rows - PATCH, cols - PATCH
-    above = permute(jnp.stack([first[:, low_row:], second[:, low_row:]]), -1, 0)
-    before = permute(jnp.stack([first[:, :, low_col:], third[:, :, low_col:]]), 0, -1)
-    corner = permute(first[:, low_row:, low_col:], -1, -1)
-    top = jnp.concatenate([corner, above[0]], axis=2)
-    bottom = jnp.concatenate([before[0], first], axis=2)
-    both = pad_lanes(jnp.concatenate([top, bottom], axis=1))
-    tall = pad_lanes(jnp.concatenate([above[1], second], axis=1))
-    broad = pad_lanes(jnp.concatenate([before[1], third], axis=2))
-    return both, tall, broad
+    planes = times * slices
+    tall_blocks, broad_blocks = rows // PATCH + 1, cols // PATCH + 1
+    both = nets[0].reshape(tall_blocks, broad_blocks, planes, PATCH, PATCH)
+    both = both.transpose(2, 0, 3, 1, 4).reshape(planes, rows + PATCH, cols + PATCH)
+    tall = nets[1].reshape(tall_blocks, times, cols, slices, PATCH)
+    tall = tall.transpose(1, 3, 0, 4, 2).reshape(planes, rows + PATCH, cols)
+    broad = nets[2].reshape(broad_blocks, times, rows, slices, PATCH)
+    broad = broad.transpose(1, 3, 2, 0, 4).reshape(planes, rows, cols + PATCH)
+    return pad_lanes(both), pad_lanes(tall), pad_lanes(broad)
 
 
 def join(offsets, weights, state, data_fit, both, tall, broad):
@@ -396,8 +428,9 @@
     )(starts, current, lows, fracs)
     chunks = jnp.transpose(sino, (1, 0, 2)).reshape(planes, tiles, agents, own)
     chunks = jnp.transpose(chunks, (1, 2, 0, 3))
-    misfit, nets = exchange(
-        chunks, measured.reshape(planes, own), patches, up_weight, down_weight
+    misfit, *nets = exchange(
+        chunks, measured.reshape(planes, own), patches, up_weight, down_weight,
+        bin_index.shape[1] // PATCH, bin_index.shape[2] // PATCH,
     )
     by_angle = jnp.transpose(misfit, (2, 0, 1, 3)).reshape(planes, angles, bins)
     by_angle = jnp.transpose(by_angle, (1, 0, 2))

time: 78.8 us -> 73.4 us (0.931); the launches traced: 77.6 us -> 73.1 us
  waiting for transfers between devices: 8.46 us -> 0.01 us
  Pallas kernels: 45 us -> 49.5 us
  starting transfers between devices: 9.96 us -> 7.82 us
  local copies, waits for them, and re-layouts: 10.9 us -> 12.1 us
    ppermute x6 -> x3, waiting for transfers between devices: 8.46 us -> 0.01 us  [permute(): return lax.ppermute(block, ('tile', 'agent'), pairs)]
    reshape x2 -> x7, local copies, waits for them, and re-layouts: 0.51 us -> 5.56 us  [the longest x2 2.47 us: spread_nets(): both = nets[0].reshape(tall_blocks, broad_blocks, planes, PATCH, PATCH)]
    pallas_call x1, Pallas kernels: 33.4 us -> 37.9 us  [exchange(): pl.pallas_call(exchange_kernel, out_shape=(jax.ShapeDtypeStruct(chunks.sh...]
    another operation x11 -> x5, local copies, waits for them, and re-layouts: 4.56 us -> 1.38 us  [the longest x3 1.19 us: make_patches(): return jnp.stack([first, second, third]).astype(jnp.bfloat16)]
    ppermute x6 -> x3, starting transfers between devices: 9.96 us -> 7.82 us  [permute(): return lax.ppermute(block, ('tile', 'agent'), pairs)]
    another operation x5 -> x4, other arithmetic: 1.25 us -> 2 us
  transfers between devices with their start and end apart: 6 -> 3, of which waited for: 1 -> 0; matrix products, arithmetic and copies ran while one was open for 3% -> 3% of each run, Pallas kernels for 6% -> 7%
where the time goes in v1:
time: 73.4 us; the launch traced here: 73.1 us
  Pallas kernels  49.5 us (67%)
  local copies, waits for them, and re-layouts  12.1 us (16%)
  starting transfers between devices  7.82 us (11%)
  other arithmetic  2.66 us (4%)
  between operations  1.06 us (1%)
    pallas_call x1, Pallas kernels, exchange(): pl.pallas_call(exchange_kernel, out_shape=(jax.ShapeDtypeStruct(chunks.sh...  37.9 us
    ppermute x3, starting transfers between devices, permute(): return lax.ppermute(block, ('tile', 'agent'), pairs)  7.82 us
    pallas_call x1, Pallas kernels, data_and_nets(): pl.pallas_call(functools.partial(project_kernel, factor, window), out_sha...  4.8 us
    pallas_call x1, Pallas kernels, data_and_nets(): pl.pallas_call(functools.partial(spread_kernel, factor, window), out_shap...  4.59 us
    reshape x2, local copies, waits for them, and re-layouts, spread_nets(): both = nets[0].reshape(tall_blocks, broad_blocks, planes, PATCH, PATCH)  2.47 us
    reshape x2, local copies, waits for them, and re-layouts, spread_nets(): both.transpose(2, 0, 3, 1, 4).reshape(planes, rows + PATCH, cols + PATCH)  2.26 us
    pallas_call x1, Pallas kernels, join(): pl.pallas_call(join_kernel, out_shape=jax.ShapeDtypeStruct(flat.shape, jn...  1.53 us
  transfers between devices with their start and end apart: 3, of which 0 were waited for; matrix products, arithmetic and copies ran while one was open for 3% of the time, Pallas kernels for 7%

profile of v1, /device:TPU:0, one launch (start us, length us, event | category | flops | bytes accessed | tf_op | source)
XLA Modules:
  0.0 73.1 jit_solution(8985706397655408788)
XLA Ops:
  0.6 0.0 copy-start
  0.6 0.0 copy-start.6
  0.7 1.2 %bitcast_convert_fusion = bf16[4,1,16,16,64]{4,3,2,0,1:T(8,128)(2,1)S(1)} fusion(f32[4,1,16,16,64]{4,3,2,1,0:T(8,128)} %param.8), kind=kLoop, calls=%fused_computation.1 | loop fusion | flops 65536 | bytes 393216 | tf_op jit(solution)/shard_map/convert.21
  1.8 0.0 slice-start
  1.8 0.0 copy-start.7
  1.9 6.4 %collective-permute-start.2 = (bf16[16,16,16]{2,1,0:T(8,128)(2,1)S(1)}, bf16[16,16,16]{2,1,0:T(8,128)(2,1)S(1)}, u32[]{:S(2)}, u32[]{:S(2)}) collective-permute-start(bf16[16,16,16]{2,1,0:T(8,128)(2,1)S(1)} %get-tuple-element.20), channel_id=1, source_target_pairs={{5,0},{6,1},{7,2},{4,3},{9,4},{10,5},{11,6},{8,7},{13,8},{14,9},{1... | collective-permute-start | bytes 24584 | tf_op jit(solution)/shard_map/ppermute | solution.py:291
  8.3 0.9 %collective-permute-start.1 = (bf16[2,16,16,64]{3,2,1,0:T(8,128)(2,1)S(1)}, bf16[2,16,16,64]{3,2,1,0:T(8,128)(2,1)S(1)}, u32[]{:S(2)}, u32[]{:S(2)}) collective-permute-start(bf16[2,16,16,64]{3,2,1,0:T(8,128)(2,1)S(1)} %slice_bitcast_fusion.1), channel_id=1, source_target_pairs={{4,0},{5,1},{6,2},{7,3},{8,4},{9,5},{10,6},{11,7},{12,8},{13,9},{1... | collective-permute-start | bytes 196616 | tf_op jit(solution)/shard_map/ppermute | solution.py:291
  9.3 0.5 collective-permute-start
  9.8 0.0 copy-done.6
  9.8 0.1 slice.63
  9.9 0.1 reshape.57.low_ref
  10.0 0.0 copy-done
  10.0 0.4 reduce_min.9
  10.4 0.0 slice-done
  10.4 0.1 reshape_squeeze.15.volume_ref
  10.5 0.0 copy-done.7
  10.5 0.1 reshape.58.frac_ref
  10.7 4.8 %project.1 = f32[16,16,512]{2,1,0:T(8,128)S(1)} custom-call(s32[16]{0:T(128)S(1)} %broadcast_minimum_fusion.starts_ref, f32[16,1024]{1,0:T(8,128)S(1)} %reshape_squeeze.15.volume_ref, s32[16,1024]{1,0:T(8,128)S(1)} %reshape.57.low_ref, s32[16,1024]{1,0:T(8,128)S(1)} %reshape.58.frac_ref), custom_call_target="tpu_custom_call" | custom-call | flops 268435456 | bytes 196608 | tf_op jit(solution)/shard_map/project/pallas_call | solution.py:420
  15.5 0.3 copy.19
  15.8 0.2 reshape.59
  16.0 0.0 copy-start.4
  16.0 0.3 copy.41
  16.4 0.0 collective-permute-done
  16.4 0.1 fusion.15.cols_ref
  16.5 0.0 collective-permute-done.1
  16.6 0.0 collective-permute-done.2
  16.6 0.1 fusion.8.both_ref
  16.7 0.0 copy-done.4
  16.7 0.7 ahead.1
  17.5 0.0 copy-start.1
  17.5 0.0 copy-start.3
  17.5 0.2 reshape_squeeze.18
  17.7 0.2 copy.42
  17.8 0.2 stack_reshape.14
  18.1 0.7 copy.25
  18.8 0.2 reshape_squeeze.16
  19.0 0.2 stack_reshape.12
  19.2 0.8 %pad_maximum_fusion.1.patches_ref = bf16[3,64,256]{2,1,0:T(8,128)(2,1)S(1)} fusion(bf16[1,64,256]{2,1,0:T(8,128)(2,1)S(1)} %stack_reshape.14, bf16[1,64,256]{2,1,0:T(8,128)(2,1)} %copy.25, bf16[1,64,256]{2,1,0:T(8,128)(2,1)S(1)} %stack_reshape.12), kind=kLoop, calls=%fused_computation.26 | loop fusion | flops 98304 | bytes 196608 | tf_op jit(solution)/shard_map/stack | solution.py:342
  20.0 0.0 copy-done.1
  20.0 0.0 copy-done.3
  20.0 0.0 copy-start.2
  20.1 1.4 %copy-done.2 = bf16[3,1024,256]{2,1,0:T(8,128)(2,1)S(1)} copy-done((bf16[3,1024,256]{2,1,0:T(8,128)(2,1)S(1)}, bf16[3,1024,256]{2,1,0:T(8,128)(2,1)}, u32[]{:S(2)}) %copy-start.2) | copy-done | bytes 1572888
  21.5 37.9 %exchange.1 = (f32[8,4,16,256]{3,2,1,0:T(8,128)S(1)}, f32[2,5,16,256]{3,2,1,0:T(8,128)S(1)}, f32[2,64,256]{2,1,0:T(8,128)S(1)}, f32[5,16,256]{2,1,0:T(8,128)S(1)}) custom-call(f32[8,4,16,256]{3,2,1,0:T(8,128)S(1)} %bitcast.75, f32[16,256]{1,0:T(8,128)S(1)} %bitcast.79, bf16[3,64,256]{2,1,0:T(8,128)(2,1)S(1)} %pad_maximum_fusion.1.patches_ref, ...), custom_call_target="tpu_custom_call" | custom-call | tf_op jit(solution)/shard_map/exchange/pallas_call | solution.py:262
  59.4 0.3 copy.26
  59.7 0.3 reshape.62
  60.0 0.3 copy.40
  60.3 4.6 %spread.1 = f32[16,1024]{1,0:T(8,128)S(1)} custom-call(s32[16]{0:T(128)S(1)} %broadcast_minimum_fusion.starts_ref, f32[16,16,512]{2,1,0:T(8,128)S(1)} %bitcast.77, s32[16,1024]{1,0:T(8,128)S(1)} %reshape.57.low_ref, s32[16,1024]{1,0:T(8,128)S(1)} %reshape.58.frac_ref, f32[16,1024]{1,0:T(8,128)S(1)} %reshape_squeeze.15.volume_ref), custom_call_target="tpu_custom_call" | custom-call | flops 268435456 | bytes 196608 | tf_op jit(solution)/shard_map/spread/pallas_call | solution.py:437
  64.9 0.1 reshape_reshape.3.fit_ref
  65.0 0.7 %reshape.70 = f32[1,16,16,64]{3,2,1,0:T(8,128)} reshape(f32[16,1024]{1,0:T(8,128)S(1)} %spread.1) | data formatting | bytes 131072 | tf_op jit(solution)/shard_map/reshape | solution.py:446
  65.7 0.4 reshape.63
  66.1 2.1 %copy.28 = f32[2,5,16,16,16]{3,0,4,1,2:T(2,128)} copy(f32[2,5,16,16,16]{4,3,2,1,0:T(8,128)S(1)} %reshape.63) | data formatting | bytes 327680 | tf_op jit(solution)/shard_map/reshape | solution.py:373
  68.2 2.1 %reshape.64 = f32[16,32,80]{1,2,0:T(8,128)S(1)} reshape(f32[16,2,16,5,16]{2,1,4,3,0:T(2,128)} %bitcast.80) | data formatting | bytes 327680 | tf_op jit(solution)/shard_map/reshape | solution.py:374
  70.3 0.2 copy.29
  70.5 0.1 copy.30
  70.7 0.2 reshape.67
  70.9 0.0 copy-start.5
  71.0 0.4 copy.39
  71.4 0.2 reshape.68
  71.6 0.0 copy-done.5
  71.6 1.5 %join.1 = f32[4,16,16,64]{3,2,1,0:T(8,128)} custom-call(s32[3]{0:T(128)S(1)} %copy-done.4, f32[4]{0:T(128)S(1)} %copy-done.5, f32[4,16,16,64]{3,2,1,0:T(8,128)S(1)} %bitcast.74, f32[16,16,64]{2,1,0:T(8,128)S(1)} %reshape_reshape.3.fit_ref, f32[16,32,128]{2,1,0:T(8,128)S(1)} %pad.33.both_ref, f32[16,32,128]{2,1,0:T(8,128)S(1)} %pad.34.rows_ref, ...), custom_call_target="tpu_custom_call" | custom-call | tf_op jit(solution)/shard_map/join/pallas_call | solution.py:387
  (18 shorter events, 0.4 us)
Async XLA Ops:
  0.6 9.3 %copy-start = (f32[4,1,16,16,64]{4,3,2,1,0:T(8,128)S(1)}, f32[4,1,16,16,64]{4,3,2,1,0:T(8,128)}, u32[]{:S(2)}) copy-start(f32[4,1,16,16,64]{4,3,2,1,0:T(8,128)} %param.8) | copy-start | bytes 786436
  0.6 9.1 %copy-start.6 = (s32[16,16,64]{2,1,0:T(8,128)S(1)}, s32[16,16,64]{2,1,0:T(8,128)}, u32[]{:S(2)}) copy-start(s32[16,16,64]{2,1,0:T(8,128)} %param.10) | copy-start | bytes 196612
  1.8 8.6 %slice-start = ((f32[4,1,16,16,64]{4,3,2,1,0:T(8,128)}), f32[1,1,16,16,64]{4,3,2,1,0:T(8,128)S(1)}, s32[]{:S(2)}) async-start(f32[4,1,16,16,64]{4,3,2,1,0:T(8,128)} %param.8), calls=%async_computation | async-start | bytes 262144 | tf_op jit(solution)/shard_map/slice | solution.py:462
  1.8 8.7 %copy-start.7 = (s32[16,16,64]{2,1,0:T(8,128)S(1)}, s32[16,16,64]{2,1,0:T(8,128)}, u32[]{:S(2)}) copy-start(s32[16,16,64]{2,1,0:T(8,128)} %param.11) | copy-start | bytes 196612
  1.9 14.7 %collective-permute-start.2 = (bf16[16,16,16]{2,1,0:T(8,128)(2,1)S(1)}, bf16[16,16,16]{2,1,0:T(8,128)(2,1)S(1)}, u32[]{:S(2)}, u32[]{:S(2)}) collective-permute-start(bf16[16,16,16]{2,1,0:T(8,128)(2,1)S(1)} %get-tuple-element.20), channel_id=1, source_target_pairs={{5,0},{6,1},{7,2},{4,3},{9,4},{10,5},{11,6},{8,7},{13,8},{14,9},{1... | collective-permute-start | bytes 24584 | tf_op jit(solution)/shard_map/ppermute | solution.py:291
  8.3 8.2 %collective-permute-start.1 = (bf16[2,16,16,64]{3,2,1,0:T(8,128)(2,1)S(1)}, bf16[2,16,16,64]{3,2,1,0:T(8,128)(2,1)S(1)}, u32[]{:S(2)}, u32[]{:S(2)}) collective-permute-start(bf16[2,16,16,64]{3,2,1,0:T(8,128)(2,1)S(1)} %slice_bitcast_fusion.1), channel_id=1, source_target_pairs={{4,0},{5,1},{6,2},{7,3},{8,4},{9,5},{10,6},{11,7},{12,8},{13,9},{1... | collective-permute-start | bytes 196616 | tf_op jit(solution)/shard_map/ppermute | solution.py:291
  9.3 7.1 %collective-permute-start = (bf16[2,16,16,16]{3,2,1,0:T(8,128)(2,1)S(1)}, bf16[2,16,16,16]{3,2,1,0:T(8,128)(2,1)S(1)}, u32[]{:S(2)}, u32[]{:S(2)}) collective-permute-start(bf16[2,16,16,16]{3,2,1,0:T(8,128)(2,1)S(1)} %pad_maximum_fusion), channel_id=1, source_target_pairs={{1,0},{2,1},{3,2},{0,3},{5,4},{6,5},{7,6},{4,7},{9,8},{10,9},{11,1... | collective-permute-start | bytes 49160 | tf_op jit(solution)/shard_map/ppermute | solution.py:291
  16.0 0.7 copy-start.4
  17.5 2.6 %copy-start.1 = (bf16[3,256,1024]{2,1,0:T(8,128)(2,1)S(1)}, bf16[3,256,1024]{2,1,0:T(8,128)(2,1)}, u32[]{:S(2)}) copy-start(bf16[3,256,1024]{2,1,0:T(8,128)(2,1)} %up_ref.1) | copy-start | bytes 4718596
  17.5 2.6 %copy-start.3 = (f32[1,16,256]{2,1,0:T(8,128)S(1)}, f32[1,16,256]{2,1,0:T(8,128)}, u32[]{:S(2)}) copy-start(f32[1,16,256]{2,1,0:T(8,128)} %param.9) | copy-start | bytes 49156
  20.0 1.4 %copy-start.2 = (bf16[3,1024,256]{2,1,0:T(8,128)(2,1)S(1)}, bf16[3,1024,256]{2,1,0:T(8,128)(2,1)}, u32[]{:S(2)}) copy-start(bf16[3,1024,256]{2,1,0:T(8,128)(2,1)} %down_ref.1) | copy-start | bytes 4718596
  70.9 0.7 copy-start.5

commit v2 on v1

--- a/solution.py
+++ b/solution.py
@@ -33,8 +33,9 @@
     return jnp.concatenate([high.astype(jnp.bfloat16), low.astype(jnp.bfloat16)], axis=0)
 
 
-def project_kernel(factor, window, starts_ref, volume_ref, low_ref, frac_ref, sino_ref):
-    angles, planes, bins = sino_ref.shape
+def project(factor, window, bins, starts_ref, volume_ref, low_ref, frac_ref, sino_ref):
+    angles, (planes, own) = low_ref.shape[0], sino_ref.shape[1:]
+    parts = bins // own
     high, low = split_pair(volume_ref[...])
     stacked = jnp.concatenate([high, low], axis=0)
 
@@ -49,20 +50,24 @@
         if bins > window:
             out = jnp.concatenate([out, jnp.zeros((planes, bins - window), jnp.float32)], axis=1)
             out = pltpu.roll(out, start, 1)
-        sino_ref[angle] = out
+        for part in range(parts):
+            sino_ref[angle * parts + part] = out[:, part * own : (part + 1) * own]
         return carry
 
     lax.fori_loop(0, angles, step, 0, unroll=4)
 
 
-def spread_kernel(factor, window, starts_ref, misfit_ref, low_ref, frac_ref, volume_ref, out_ref):
-    angles, planes, bins = misfit_ref.shape
+def spread(factor, window, bins, starts_ref, misfit_ref, low_ref, frac_ref, volume_ref, out_ref):
+    angles, (planes, own) = low_ref.shape[0], misfit_ref.shape[1:]
+    parts = bins // own
     out_ref[...] = volume_ref[...]
 
     def step(angle, carry):
         start = starts_ref[angle]
         rows = interpolation_rows(low_ref, frac_ref, angle, start, window)
-        resid = misfit_ref[angle]
+        resid = jnp.concatenate(
+            [misfit_ref[angle * parts + part] for part in range(parts)], axis=1
+        )
         if bins > window:
             resid = pltpu.roll(resid, bins - start, 1)[:, :window]
         high, low = split_pair(resid)
@@ -76,15 +81,17 @@
 
 
 def exchange_kernel(
-    chunks_ref, target_ref, patches_ref, up_ref, down_ref,
-    misfit_ref, both_ref, rows_ref, cols_ref,
-    tile_parts, band, agent_parts, every, wide, terms, term_parts,
+    factor, window, bins, agents,
+    starts_ref, volume_ref, low_ref, frac_ref, target_ref, patches_ref, up_ref, down_ref,
+    fit_ref, both_ref, rows_ref, cols_ref,
+    chunks, tile_parts, band, agent_parts, every, wide, terms, term_parts,
     tile_send, tile_recv, sum_send, sum_recv, own_send, own_recv,
     every_send, every_recv, patch_send, patch_recv, term_send, term_recv,
     edge_send, edge_recv,
 ):
-    tiles, agents = chunks_ref.shape[0], chunks_ref.shape[1]
+    tiles = chunks.shape[0] // agents
     tile, agent = lax.axis_index("tile"), lax.axis_index("agent")
+    mine = tile * agents + agent
 
     def tile_at(step):
         return lax.rem(tile + step, tiles)
@@ -102,6 +109,9 @@
             device_id_type=pl.DeviceIdType.MESH,
         )
 
+    def share_of(which):
+        return pl.ds(which * agents, agents)
+
     def to_tile(step):
         return (tile_at(step), agent)
 
@@ -127,7 +137,7 @@
 
     def tile_copy(step):
         return copy(
-            chunks_ref.at[tile_at(step)], tile_parts.at[step], tile_send, tile_recv, step,
+            chunks.at[share_of(tile_at(step))], tile_parts.at[step], tile_send, tile_recv, step,
             to_tile(step))
 
     def patch_copy(which):
@@ -142,19 +152,19 @@
 
     def own_copy(step):
         return copy(
-            every.at[tile, agent], every.at[tile, agent], own_send, own_recv, step,
+            every.at[mine], every.at[mine], own_send, own_recv, step,
             to_agent(step))
 
     def own_arrival(step):
-        where = every.at[tile, agent_at(agents - step)]
+        where = every.at[tile * agents + agent_at(agents - step)]
         return copy(where, where, own_send, own_recv, step, to_agent(step))
 
     def every_copy(step):
         return copy(
-            every.at[tile], every.at[tile], every_send, every_recv, step, to_tile(step))
+            every.at[share_of(tile)], every.at[share_of(tile)], every_send, every_recv, step, to_tile(step))
 
     def every_arrival(step):
-        where = every.at[tile_at(tiles - step)]
+        where = every.at[share_of(tile_at(tiles - step))]
         return copy(where, where, every_send, every_recv, step, to_tile(step))
 
     def term_copy(which):
@@ -163,29 +173,9 @@
             term_recv.at[which], step, to_agent(step))
 
     nets = range(patches_ref.shape[0])
-    over(tiles, lambda step: tile_copy(step).start())
-    for which in nets:
-        over(agents, lambda step: patch_copy(which)(step).start())
-        wide[which, 0] = patches_ref[which]
-    band[...] = chunks_ref[tile]
-
-    def add_tile(step):
-        tile_copy(step).wait_recv()
-        band[...] += tile_parts[step]
-
-    over(tiles, add_tile)
-    over(agents, lambda step: sum_copy(step).start())
-    every[tile, agent] = band[agent] - target_ref[...]
-
-    def add_agent(step):
-        sum_copy(step).wait_recv()
-        every[tile, agent] += agent_parts[step]
-
-    over(agents, add_agent)
-    over(agents, lambda step: own_copy(step).start())
-
     count = patches_ref.shape[1]
-    for which in nets:
+
+    def run_net(which):
         over(agents, lambda step: patch_copy(which)(step).wait_recv())
         rows = wide[which].reshape(agents * count, patches_ref.shape[2])
         hidden = jnp.dot(rows, up_ref[which], preferred_element_type=jnp.float32)
@@ -194,10 +184,32 @@
         terms[which] = out.reshape(agents, count, out.shape[1])
         over(agents, lambda step: term_copy(which)(step).start())
 
+    def add_tile(step):
+        tile_copy(step).wait_recv()
+        band[...] += tile_parts[step]
+
+    def add_agent(step):
+        sum_copy(step).wait_recv()
+        every[mine] += agent_parts[step]
+
+    for which in nets:
+        over(agents, lambda step: patch_copy(which)(step).start())
+        wide[which, 0] = patches_ref[which]
+    project(factor, window, bins, starts_ref, volume_ref, low_ref, frac_ref, chunks)
+    over(tiles, lambda step: tile_copy(step).start())
+    band[...] = chunks[share_of(tile)]
+    run_net(0)
+    over(tiles, add_tile)
+    over(agents, lambda step: sum_copy(step).start())
+    every[mine] = band[agent] - target_ref[...]
+    run_net(1)
+    over(agents, add_agent)
+    over(agents, lambda step: own_copy(step).start())
+    run_net(2)
     over(agents, lambda step: own_arrival(step).wait_recv())
     over(tiles, lambda step: every_copy(step).start())
     over(tiles, lambda step: every_arrival(step).wait_recv())
-    misfit_ref[...] = every[...]
+    spread(factor, window, bins, starts_ref, every, low_ref, frac_ref, volume_ref, fit_ref)
     row_blocks, col_blocks = both_ref.shape[0] - 1, both_ref.shape[1] - 1
     next_tile, next_agent = to_tile(1), to_agent(1)
     across = (next_tile[0], next_agent[1])
@@ -244,8 +256,13 @@
     over(tiles, lambda step: every_copy(step).wait_send())
 
 
-def exchange(chunks, target, patches, up_weight, down_weight, row_blocks, col_blocks):
-    tiles, agents, planes, own = chunks.shape
+def exchange(
+    factor, window, starts, volume, lows, fracs, target, patches, up_weight, down_weight, blocks
+):
+    tiles, agents = lax.axis_size("tile"), lax.axis_size("agent")
+    planes, own = target.shape
+    row_blocks, col_blocks = blocks
+    bins = tiles * agents * own // lows.shape[0]
     whole = pl.BlockSpec(memory_space=pltpu.VMEM)
     count, pixels = patches.shape[1:]
     shapes = (
@@ -260,15 +277,16 @@
     sems += [pltpu.SemaphoreType.DMA((5,))] * 2
     by_net = (patches.shape[0], agents) + patches.shape[1:]
     return pl.pallas_call(
-        exchange_kernel,
-        out_shape=(jax.ShapeDtypeStruct(chunks.shape, jnp.float32),) + parts,
-        in_specs=[whole] * 5,
+        functools.partial(exchange_kernel, factor, window, bins, agents),
+        out_shape=(jax.ShapeDtypeStruct(volume.shape, jnp.float32),) + parts,
+        in_specs=[pl.BlockSpec(memory_space=pltpu.SMEM)] + [whole] * 7,
         out_specs=(whole,) * 4,
         scratch_shapes=[
-            pltpu.VMEM(chunks.shape, jnp.float32),
+            pltpu.VMEM((tiles * agents, planes, own), jnp.float32),
+            pltpu.VMEM((tiles, agents, planes, own), jnp.float32),
             pltpu.VMEM((agents, planes, own), jnp.float32),
             pltpu.VMEM((agents, planes, own), jnp.float32),
-            pltpu.VMEM(chunks.shape, jnp.float32),
+            pltpu.VMEM((tiles * agents, planes, own), jnp.float32),
             pltpu.VMEM(by_net, jnp.bfloat16),
             pltpu.VMEM(by_net, jnp.float32),
             pltpu.VMEM(by_net, jnp.float32),
@@ -278,7 +296,7 @@
             collective_id=0, has_side_effects=True, vmem_limit_bytes=48 * 2**20
         ),
         name="exchange",
-    )(chunks, target, patches, up_weight, down_weight)
+    )(starts, volume, lows, fracs, target, patches, up_weight, down_weight)
 
 
 def permute(block, step_tile, step_agent):
@@ -370,8 +388,12 @@
     times, slices, rows, cols = shape
     planes = times * slices
     tall_blocks, broad_blocks = rows // PATCH + 1, cols // PATCH + 1
-    both = nets[0].reshape(tall_blocks, broad_blocks, planes, PATCH, PATCH)
-    both = both.transpose(2, 0, 3, 1, 4).reshape(planes, rows + PATCH, cols + PATCH)
+
+    def in_columns(block):
+        block = block.reshape(tall_blocks, -1, planes, PATCH, PATCH)
+        return block.transpose(2, 0, 3, 1, 4).reshape(planes, rows + PATCH, -1)
+
+    both = jnp.concatenate([in_columns(nets[0][:, :1]), in_columns(nets[0][:, 1:])], axis=2)
     tall = nets[1].reshape(tall_blocks, times, cols, slices, PATCH)
     tall = tall.transpose(1, 3, 0, 4, 2).reshape(planes, rows + PATCH, cols)
     broad = nets[2].reshape(broad_blocks, times, rows, slices, PATCH)
@@ -409,40 +431,10 @@
     fracs = bin_frac.reshape(angles, -1)
     corners = bin_index[:, :: bin_index.shape[1] - 1, :: bin_index.shape[2] - 1]
     starts = jnp.minimum(jnp.min(corners, axis=(1, 2)), bins - window)
-    whole = pl.BlockSpec(memory_space=pltpu.VMEM)
-    scalars = pl.BlockSpec(memory_space=pltpu.SMEM)
-    cost = pl.CostEstimate(
-        flops=4 * angles * window * current.shape[1] * planes * 2,
-        bytes_accessed=3 * current.size * 4,
-        transcendentals=0,
-    )
-    grant = pltpu.CompilerParams(vmem_limit_bytes=48 * 2**20)
-    sino = pl.pallas_call(
-        functools.partial(project_kernel, factor, window),
-        out_shape=jax.ShapeDtypeStruct((angles, planes, bins), jnp.float32),
-        in_specs=[scalars, whole, whole, whole],
-        out_specs=whole,
-        cost_estimate=cost,
-        compiler_params=grant,
-        name="project",
-    )(starts, current, lows, fracs)
-    chunks = jnp.transpose(sino, (1, 0, 2)).reshape(planes, tiles, agents, own)
-    chunks = jnp.transpose(chunks, (1, 2, 0, 3))
-    misfit, *nets = exchange(
-        chunks, measured.reshape(planes, own), patches, up_weight, down_weight,
-        bin_index.shape[1] // PATCH, bin_index.shape[2] // PATCH,
-    )
-    by_angle = jnp.transpose(misfit, (2, 0, 1, 3)).reshape(planes, angles, bins)
-    by_angle = jnp.transpose(by_angle, (1, 0, 2))
-    result = pl.pallas_call(
-        functools.partial(spread_kernel, factor, window),
-        out_shape=jax.ShapeDtypeStruct(current.shape, jnp.float32),
-        in_specs=[scalars, whole, whole, whole, whole],
-        out_specs=whole,
-        cost_estimate=cost,
-        compiler_params=grant,
-        name="spread",
-    )(starts, by_angle, lows, fracs, current)
+    result, *nets = exchange(
+        factor, window, starts, current, lows, fracs, measured.reshape(planes, own), patches,
+        up_weight, down_weight, (bin_index.shape[1] // PATCH, bin_index.shape[2] // PATCH),
+    )
     return result.reshape(volume.shape), nets
 
 

time: 73.4 us -> 72.5 us (0.988)
  local copies, waits for them, and re-layouts: 12.1 us -> 8.98 us
  waiting for transfers between devices: 0.01 us -> 1.99 us
  Pallas kernels: 49.5 us -> 50.5 us
    reshape x8 -> x5, local copies, waits for them, and re-layouts: 5.87 us -> 3.81 us  [the longest x4 3.34 us: in_columns(): block = block.reshape(tall_blocks, -1, planes, PATCH, PATCH)]
    ppermute x3, waiting for transfers between devices: 0.01 us -> 1.99 us  [permute(): return lax.ppermute(block, ('tile', 'agent'), pairs)]
    pallas_call x3 -> x1, Pallas kernels: 47.3 us -> 48.2 us  [exchange(): pl.pallas_call(functools.partial(exchange_kernel, factor, window, bins, a...]
    another operation x1, other arithmetic: 0.77 us -> 0.01 us  [make_patches(): return jnp.stack([first, second, third]).astype(jnp.bfloat16)]
  transfers between devices with their start and end apart: 3 -> 3, of which waited for: 0 -> 1; matrix products, arithmetic and copies ran while one was open for 3% -> 1% of each run, Pallas kernels for 7% -> 0%
where the time goes in v2:
time: 72.5 us; the launch traced here: 72.2 us
  Pallas kernels  50.5 us (70%)
  local copies, waits for them, and re-layouts  8.98 us (12%)
  starting transfers between devices  7.77 us (11%)
  other arithmetic  2.02 us (3%)
  waiting for transfers between devices  1.99 us (3%)
  between operations  1 us (1%)
    pallas_call x1, Pallas kernels, exchange(): pl.pallas_call(functools.partial(exchange_kernel, factor, window, bins, a...  48.2 us
    ppermute x3, starting transfers between devices, permute(): return lax.ppermute(block, ('tile', 'agent'), pairs)  7.77 us
    reshape x4, local copies, waits for them, and re-layouts, in_columns(): block = block.reshape(tall_blocks, -1, planes, PATCH, PATCH)  3.34 us
    ppermute x3, waiting for transfers between devices, permute(): return lax.ppermute(block, ('tile', 'agent'), pairs)  1.99 us
    unnamed x16, local copies, waits for them, and re-layouts  1.74 us
    pallas_call x1, Pallas kernels, join(): pl.pallas_call(join_kernel, out_shape=jax.ShapeDtypeStruct(flat.shape, jn...  1.53 us
  transfers between devices with their start and end apart: 3, of which 1 were waited for; matrix products, arithmetic and copies ran while one was open for 1% of the time, Pallas kernels for 0%

profile of v2, /device:TPU:0, one launch (start us, length us, event | category | flops | bytes accessed | tf_op | source)
XLA Modules:
  0.0 72.2 jit_solution(335753523330770060)
XLA Ops:
  0.6 0.0 copy-start
  0.6 0.0 copy-start.6
  0.7 1.1 %bitcast_convert_fusion = bf16[4,1,16,16,64]{4,3,2,0,1:T(8,128)(2,1)S(1)} fusion(f32[4,1,16,16,64]{4,3,2,1,0:T(8,128)} %param.8), kind=kLoop, calls=%fused_computation.2 | loop fusion | flops 65536 | bytes 393216 | tf_op jit(solution)/shard_map/convert.21
  1.8 0.0 slice-start
  1.8 0.0 copy-start.7
  1.9 5.1 %collective-permute-start = (bf16[2,16,16,16]{3,2,1,0:T(8,128)(2,1)S(1)}, bf16[2,16,16,16]{3,2,1,0:T(8,128)(2,1)S(1)}, u32[]{:S(2)}, u32[]{:S(2)}) collective-permute-start(bf16[2,16,16,16]{3,2,1,0:T(8,128)(2,1)S(1)} %pad_maximum_fusion), channel_id=1, source_target_pairs={{1,0},{2,1},{3,2},{0,3},{5,4},{6,5},{7,6},{4,7},{9,8},{10,9},{11,1... | collective-permute-start | bytes 49160 | tf_op jit(solution)/shard_map/ppermute | solution.py:309
  7.0 1.5 %collective-permute-start.2 = (bf16[16,16,16]{2,1,0:T(8,128)(2,1)S(1)}, bf16[16,16,16]{2,1,0:T(8,128)(2,1)S(1)}, u32[]{:S(2)}, u32[]{:S(2)}) collective-permute-start(bf16[16,16,16]{2,1,0:T(8,128)(2,1)S(1)} %get-tuple-element.20), channel_id=1, source_target_pairs={{5,0},{6,1},{7,2},{4,3},{9,4},{10,5},{11,6},{8,7},{13,8},{14,9},{1... | collective-permute-start | bytes 24584 | tf_op jit(solution)/shard_map/ppermute | solution.py:309
  8.5 1.2 %collective-permute-start.1 = (bf16[2,16,16,64]{3,2,1,0:T(8,128)(2,1)S(1)}, bf16[2,16,16,64]{3,2,1,0:T(8,128)(2,1)S(1)}, u32[]{:S(2)}, u32[]{:S(2)}) collective-permute-start(bf16[2,16,16,64]{3,2,1,0:T(8,128)(2,1)S(1)} %slice_bitcast_fusion.1), channel_id=1, source_target_pairs={{4,0},{5,1},{6,2},{7,3},{8,4},{9,5},{10,6},{11,7},{12,8},{13,9},{1... | collective-permute-start | bytes 196616 | tf_op jit(solution)/shard_map/ppermute | solution.py:309
  9.7 0.0 copy-done
  9.7 0.0 copy-start.4
  9.8 0.0 copy-done.6
  9.8 0.1 slice.69
  9.9 0.4 reduce_min.9
  10.3 0.1 reshape.57.low_ref
  10.4 0.0 slice-done
  10.4 0.1 reshape_squeeze.15.volume_ref
  10.5 0.0 copy-done.7
  10.5 0.1 reshape.58.frac_ref
  10.6 0.0 collective-permute-done
  10.6 0.1 fusion.15.cols_ref
  10.7 2.0 %collective-permute-done.1 = bf16[2,16,16,64]{3,2,1,0:T(8,128)(2,1)S(1)} collective-permute-done((bf16[2,16,16,64]{3,2,1,0:T(8,128)(2,1)S(1)}, bf16[2,16,16,64]{3,2,1,0:T(8,128)(2,1)S(1)}, u32[]{:S(2)}, u32[]{:S(2)}) %collective-permute-start.1) | collective-permute-done | bytes 65568 | tf_op jit(solution)/shard_map/ppermute | solution.py:309
  12.8 0.0 collective-permute-done.2
  12.8 0.1 fusion.8.both_ref
  12.9 0.0 copy-done.4
  12.9 0.7 ahead.1
  13.7 0.0 copy-start.1
  13.7 0.0 copy-start.3
  13.7 0.2 reshape_squeeze.16
  13.9 0.2 stack_reshape.12
  14.2 0.2 reshape_squeeze.18
  14.3 0.2 copy.37
  14.5 0.2 stack_reshape.14
  14.7 0.1 copy.24
  14.9 0.2 copy-done.1
  15.1 0.0 copy-done.3
  15.1 0.0 copy-start.2
  15.1 1.4 %copy-done.2 = bf16[3,1024,256]{2,1,0:T(8,128)(2,1)S(1)} copy-done((bf16[3,1024,256]{2,1,0:T(8,128)(2,1)S(1)}, bf16[3,1024,256]{2,1,0:T(8,128)(2,1)}, u32[]{:S(2)}) %copy-start.2) | copy-done | bytes 1572888
  16.5 48.2 %exchange.1 = (f32[16,1024]{1,0:T(8,128)S(1)}, f32[2,5,16,256]{3,2,1,0:T(8,128)S(1)}, f32[2,64,256]{2,1,0:T(8,128)S(1)}, f32[5,16,256]{2,1,0:T(8,128)S(1)}) custom-call(s32[16]{0:T(128)S(1)} %broadcast_minimum_fusion.starts_ref, f32[16,1024]{1,0:T(8,128)S(1)} %reshape_squeeze.15.volume_ref, s32[16,1024]{1,0:T(8,128)S(1)} %reshape.57.low_ref, ...), custom_call_target="tpu_custom_call" | custom-call | tf_op jit(solution)/shard_map/exchange/pallas_call | solution.py:279
  64.8 0.1 reshape_reshape.3.fit_ref
  64.8 0.7 %reshape.70 = f32[1,16,16,64]{3,2,1,0:T(8,128)} reshape(f32[16,1024]{1,0:T(8,128)S(1)} %get-tuple-element.6) | data formatting | bytes 131072 | tf_op jit(solution)/shard_map/reshape | solution.py:438
  65.6 1.3 %reshape.63 = f32[2,4,16,16,16]{4,3,2,1,0:T(8,128)} reshape(f32[2,4,16,256]{3,2,1,0:T(8,128)S(1)} %slice.87) | data formatting | bytes 262144 | tf_op jit(solution)/shard_map/reshape | solution.py:393
  66.9 1.9 %copy.36 = f32[2,4,16,16,16]{4,1,3,0,2:T(4,128)S(1)} copy(f32[2,4,16,16,16]{4,3,2,1,0:T(8,128)} %reshape.63) | data formatting | bytes 262144 | tf_op jit(solution)/shard_map/reshape | solution.py:393
  68.8 0.5 reshape.64
  69.3 0.1 reshape.61
  69.4 0.2 reshape.67
  69.6 0.4 copy.35
  70.1 0.0 copy-start.5
  70.1 0.2 reshape.68
  70.3 0.1 copy.27
  70.5 0.1 select_maximum_fusion.both_ref
  70.6 0.1 copy-done.5
  70.7 1.5 %join.1 = f32[4,16,16,64]{3,2,1,0:T(8,128)} custom-call(s32[3]{0:T(128)S(1)} %copy-done.4, f32[4]{0:T(128)S(1)} %copy-done.5, f32[4,16,16,64]{3,2,1,0:T(8,128)S(1)} %bitcast.71, f32[16,16,64]{2,1,0:T(8,128)S(1)} %reshape_reshape.3.fit_ref, f32[16,32,128]{2,1,0:T(8,128)S(1)} %select_maximum_fusion.both_ref, f32[16,32,128]{2,1,0:T(8,128)S(1)} %pad.34.rows_ref, ...), custom_call_target="tpu_custom_call" | custom-call | tf_op jit(solution)/shard_map/join/pallas_call | solution.py:409
  (21 shorter events, 0.4 us)
Async XLA Ops:
  0.6 9.1 %copy-start = (f32[4,1,16,16,64]{4,3,2,1,0:T(8,128)S(1)}, f32[4,1,16,16,64]{4,3,2,1,0:T(8,128)}, u32[]{:S(2)}) copy-start(f32[4,1,16,16,64]{4,3,2,1,0:T(8,128)} %param.8) | copy-start | bytes 786436
  0.6 9.1 %copy-start.6 = (s32[16,16,64]{2,1,0:T(8,128)S(1)}, s32[16,16,64]{2,1,0:T(8,128)}, u32[]{:S(2)}) copy-start(s32[16,16,64]{2,1,0:T(8,128)} %param.10) | copy-start | bytes 196612
  1.8 8.6 %slice-start = ((f32[4,1,16,16,64]{4,3,2,1,0:T(8,128)}), f32[1,1,16,16,64]{4,3,2,1,0:T(8,128)S(1)}, s32[]{:S(2)}) async-start(f32[4,1,16,16,64]{4,3,2,1,0:T(8,128)} %param.8), calls=%async_computation | async-start | bytes 262144 | tf_op jit(solution)/shard_map/slice | solution.py:454
  1.8 8.7 %copy-start.7 = (s32[16,16,64]{2,1,0:T(8,128)S(1)}, s32[16,16,64]{2,1,0:T(8,128)}, u32[]{:S(2)}) copy-start(s32[16,16,64]{2,1,0:T(8,128)} %param.11) | copy-start | bytes 196612
  1.9 8.7 %collective-permute-start = (bf16[2,16,16,16]{3,2,1,0:T(8,128)(2,1)S(1)}, bf16[2,16,16,16]{3,2,1,0:T(8,128)(2,1)S(1)}, u32[]{:S(2)}, u32[]{:S(2)}) collective-permute-start(bf16[2,16,16,16]{3,2,1,0:T(8,128)(2,1)S(1)} %pad_maximum_fusion), channel_id=1, source_target_pairs={{1,0},{2,1},{3,2},{0,3},{5,4},{6,5},{7,6},{4,7},{9,8},{10,9},{11,1... | collective-permute-start | bytes 49160 | tf_op jit(solution)/shard_map/ppermute | solution.py:309
  7.0 5.8 %collective-permute-start.2 = (bf16[16,16,16]{2,1,0:T(8,128)(2,1)S(1)}, bf16[16,16,16]{2,1,0:T(8,128)(2,1)S(1)}, u32[]{:S(2)}, u32[]{:S(2)}) collective-permute-start(bf16[16,16,16]{2,1,0:T(8,128)(2,1)S(1)} %get-tuple-element.20), channel_id=1, source_target_pairs={{5,0},{6,1},{7,2},{4,3},{9,4},{10,5},{11,6},{8,7},{13,8},{14,9},{1... | collective-permute-start | bytes 24584 | tf_op jit(solution)/shard_map/ppermute | solution.py:309
  8.5 4.2 %collective-permute-start.1 = (bf16[2,16,16,64]{3,2,1,0:T(8,128)(2,1)S(1)}, bf16[2,16,16,64]{3,2,1,0:T(8,128)(2,1)S(1)}, u32[]{:S(2)}, u32[]{:S(2)}) collective-permute-start(bf16[2,16,16,64]{3,2,1,0:T(8,128)(2,1)S(1)} %slice_bitcast_fusion.1), channel_id=1, source_target_pairs={{4,0},{5,1},{6,2},{7,3},{8,4},{9,5},{10,6},{11,7},{12,8},{13,9},{1... | collective-permute-start | bytes 196616 | tf_op jit(solution)/shard_map/ppermute | solution.py:309
  9.7 3.2 %copy-start.4 = (s32[3]{0:T(128)S(1)}, s32[3]{0:T(128)}, u32[]{:S(2)}) copy-start(s32[3]{0:T(128)} %offsets_ref.3) | copy-start | bytes 40
  13.7 1.4 %copy-start.1 = (bf16[3,256,1024]{2,1,0:T(8,128)(2,1)S(1)}, bf16[3,256,1024]{2,1,0:T(8,128)(2,1)}, u32[]{:S(2)}) copy-start(bf16[3,256,1024]{2,1,0:T(8,128)(2,1)} %up_ref.1) | copy-start | bytes 4718596
  13.7 1.4 %copy-start.3 = (f32[1,16,256]{2,1,0:T(8,128)S(1)}, f32[1,16,256]{2,1,0:T(8,128)}, u32[]{:S(2)}) copy-start(f32[1,16,256]{2,1,0:T(8,128)} %param.9) | copy-start | bytes 49156
  15.1 1.4 %copy-start.2 = (bf16[3,1024,256]{2,1,0:T(8,128)(2,1)S(1)}, bf16[3,1024,256]{2,1,0:T(8,128)(2,1)}, u32[]{:S(2)}) copy-start(bf16[3,1024,256]{2,1,0:T(8,128)(2,1)} %down_ref.1) | copy-start | bytes 4718596
  70.1 0.7 copy-start.5
